TPU v7x, 32 devices: a whole 2x2x4 slice. The times are simulated.
32 devices in a mesh: row: 8 (over z, x), col: 4 (over y, core).
Axes of the slice: x: 2, y: 2, z: 4, core: 2. Of those that a mesh axis runs over, the one named last changes fastest.
Arguments:
- features: float32 [6144, 64], P('row'), may hold values from -6 to 6
- noise: float32 [6144], P('row'), may hold values from 0.1 to 1
- tile_map: int32 [48], replicated, may hold values from 0 to 47, each once
- panel_tile: int32 [1], replicated, may hold values from 0 to 35
Outputs:
- panel: float32 [6144, 128], P('row')
- trailing: float32 [6144, 6144], P('row', 'col')
Inputs may be any that keep to these rules, and one draw needn't show every extreme that they name: `tile_map`: a permutation: every global tile 0 to 47 is held by exactly one slot.
All inputs are finite; a program needn't handle non-finite values.
Results may differ from a plain program's by a relative error of at most 0.0003.
Values sent between devices are 32-bit elements; how exact they have to be, the bound alone decides.
A program may use at most 64 MiB of HBM per device.

v0:
```python
import functools

import jax
import jax.numpy as jnp
from jax import lax
from jax.experimental import pallas as pl
from jax.experimental.pallas import tpu as pltpu
from jax.sharding import PartitionSpec as P

TILE = 128
FEAT = 64
CAND = 72
DEPTH = 6 * FEAT + 16
BLOCK = 32
HIGHEST = lax.Precision.HIGHEST
MESH = pl.DeviceIdType.MESH
CONTRACT_FIRST = (((0,), (0,)), ((), ()))
CONTRACT_LAST = (((1,), (1,)), ((), ()))


def split3(x):
    hi = x.astype(jnp.bfloat16)
    rest = x - hi.astype(jnp.float32)
    mid = rest.astype(jnp.bfloat16)
    lo = (rest - mid.astype(jnp.float32)).astype(jnp.bfloat16)
    return hi, mid, lo


def norm_rows(f, first):
    sq = jnp.sum(f * f, axis=0, keepdims=True) * (-1.0 / FEAT)
    parts = [p.astype(jnp.float32) for p in split3(sq)]
    row = lax.broadcasted_iota(jnp.int32, (16, f.shape[1]), 0)
    out = jnp.zeros((16, f.shape[1]), jnp.float32)
    for k in range(3):
        out = jnp.where(row == first + k, parts[k], out)
        out = jnp.where(row == 3 - first + k, 1.0, out)
    return out.astype(jnp.bfloat16)


def left_terms(f):
    hi, mid, lo = split3(f * (2.0 / FEAT))
    return jnp.concatenate([hi, hi, mid, mid, hi, lo, norm_rows(f, 0)], axis=0)


def right_terms(f):
    hi, mid, lo = split3(f)
    return jnp.concatenate([hi, mid, hi, mid, lo, hi, norm_rows(f, 3)], axis=0)


def exponent(left, right):
    return lax.dot_general(left, right, CONTRACT_FIRST, preferred_element_type=jnp.float32)


def eliminate(table, between=None):
    lane = lax.broadcasted_iota(jnp.int32, (1, TILE), 1)
    sub = lax.broadcasted_iota(jnp.int32, (8, 1), 0)
    block_lane = lax.broadcasted_iota(jnp.int32, (BLOCK, TILE), 1)
    block_sub = lax.broadcasted_iota(jnp.int32, (BLOCK, TILE), 0)
    done = []
    below = table
    for k in range(TILE // BLOCK):
        groups = [below[g * 8 : g * 8 + 8] for g in range(BLOCK // 8)]
        pieces = []
        for j in range(BLOCK):
            at = k * BLOCK + j
            g, o = j // 8, j % 8
            row = groups[g][o : o + 1]
            pivot = row[:, at : at + 1]
            unit = jnp.where(lane == at, 1.0, row)
            pieces.append(unit / jnp.sqrt(pivot))
            scaled = unit / pivot
            for h in range(g, BLOCK // 8):
                col = groups[h][:, at : at + 1]
                if h == g:
                    col = jnp.where(sub > o, col, 0.0)
                    keep = (lane != at) | (sub <= o)
                else:
                    keep = lane != at
                groups[h] = jnp.where(keep, groups[h], 0.0) - col * scaled
            if between is not None and j % 8 == 7:
                between(at // 8)
        block = jnp.concatenate(pieces, axis=0)
        lower = block_lane <= block_sub + k * BLOCK
        done.append(jnp.where(lower, block, 0.0))
        if (k + 1) * BLOCK < TILE:
            own = (lane >= k * BLOCK) & (lane < (k + 1) * BLOCK)
            right = jnp.where(lower | (block_lane >= (k + 1) * BLOCK), block, 0.0)
            update = lax.dot_general(
                block, right, CONTRACT_FIRST, precision=HIGHEST, preferred_element_type=jnp.float32
            )
            below = jnp.where(own, 0.0, below[BLOCK:]) - update[(k + 1) * BLOCK :]
    return jnp.concatenate(done, axis=0)


CHUNKS = 4


def gather_kernel(
    lines, across, cols, tiles, map_hbm, panel_hbm, feat_hbm, noise_hbm,
    left_out, noise_out, here_out, there_out, pivot_out, inverse_out, pleft_out, pright_out, col_ref,
    map_ref, panel_ref, feat_ref, own_ref, sum_ref, near_ref, far_ref,
    in_sem, near_send, near_recv, far_send, far_recv, line_send, line_recv, side_send, side_recv, local_sem,
):
    r = lax.axis_index("row")
    c = lax.axis_index("col")
    rows = lines * across
    per_col = rows // cols
    z = r // across
    x = lax.rem(r, across)
    loads = [
        pltpu.make_async_copy(src, dst, in_sem.at[n])
        for n, (src, dst) in enumerate(
            [(map_hbm, map_ref), (panel_hbm, panel_ref), (feat_hbm, feat_ref), (noise_hbm, noise_out)]
        )
    ]
    for load in loads:
        load.start()
    barrier = pltpu.get_barrier_semaphore()
    for d in range(1, rows):
        pl.semaphore_signal(
            barrier, inc=1, device_id={"row": lax.rem(r + d, rows)}, device_id_type=MESH
        )
    for load in loads:
        load.wait()
    pivot_tile = panel_ref[0]
    feat = jnp.zeros((FEAT, TILE), jnp.float32)
    noise = jnp.zeros((1, TILE), jnp.float32)
    for s in range(tiles):
        held = map_ref[r * tiles + s] == pivot_tile
        feat = jnp.where(held, feat_ref[:, s * TILE : (s + 1) * TILE], feat)
        noise = jnp.where(held, noise_out[s : s + 1, :], noise)
    own_ref[:FEAT] = feat
    own_ref[FEAT:] = jnp.broadcast_to(noise, (CAND - FEAT, TILE))
    pl.semaphore_wait(barrier, rows - 1)

    def near(d, src, dst):
        return pltpu.make_async_remote_copy(
            src_ref=own_ref, dst_ref=near_ref.at[d - 1],
            send_sem=near_send.at[d - 1], recv_sem=near_recv.at[d - 1],
            device_id={"row": z * across + lax.rem(x + d, across)}, device_id_type=MESH,
        )

    def far(d):
        return pltpu.make_async_remote_copy(
            src_ref=sum_ref, dst_ref=far_ref.at[d - 1],
            send_sem=far_send.at[d - 1], recv_sem=far_recv.at[d - 1],
            device_id={"row": lax.rem(z + d, lines) * across + x}, device_id_type=MESH,
        )

    nears = [near(d, None, None) for d in range(1, across)]
    fars = [far(d) for d in range(1, lines)]
    for copy in nears:
        copy.start()
    for s in range(tiles):
        left_out[:, s * TILE : (s + 1) * TILE] = left_terms(feat_ref[:, s * TILE : (s + 1) * TILE])
        here_out[s * 8 : s * 8 + 8] = jnp.full((8, TILE), map_ref[r * tiles + s], jnp.int32)
    for t in range(per_col * tiles):
        there_out[:, t * TILE : (t + 1) * TILE] = jnp.full(
            (8, TILE), map_ref[c * per_col * tiles + t], jnp.int32
        )
    pivot_out[...] = jnp.full((8, TILE), pivot_tile, jnp.int32)
    for copy in nears:
        copy.wait_recv()
    total = own_ref[...]
    for d in range(1, across):
        total += near_ref[d - 1]
    sum_ref[...] = total
    for copy in fars:
        copy.start()
    for copy in fars:
        copy.wait_recv()
    for d in range(1, lines):
        total += far_ref[d - 1]

    first = c * per_col
    source_z = first // across
    first_x = lax.rem(first, across)
    member = x - first_x
    on_line = (member >= 0) & (member < per_col)
    slot = jnp.clip(member, 0, per_col - 1)
    hop = jnp.abs(z - source_z)
    rows_each = FEAT // CHUNKS

    def chunk(q):
        return col_ref.at[slot, pl.ds(q * rows_each, rows_each)]

    def line_copy(q, side):
        to = jnp.clip(z + (1 if side == 0 else -1), 0, lines - 1)
        return pltpu.make_async_remote_copy(
            src_ref=chunk(q), dst_ref=chunk(q),
            send_sem=line_send.at[side, q], recv_sem=line_recv.at[q],
            device_id={"row": to * across + x}, device_id_type=MESH,
        )

    def side_copy(q, d):
        return pltpu.make_async_remote_copy(
            src_ref=chunk(q), dst_ref=chunk(q),
            send_sem=side_send.at[d - 1, q], recv_sem=side_recv.at[slot, q],
            device_id={"row": z * across + lax.rem(x + d, across)}, device_id_type=MESH,
        )

    up = on_line & (z >= source_z) & (z < lines - 1)
    down = on_line & (z <= source_z) & (z > 0)

    def pass_on(q):
        @pl.when(up)
        def _():
            line_copy(q, 0).start()

        @pl.when(down)
        def _():
            line_copy(q, 1).start()

        for d in range(1, across):
            side_copy(q, d).start()

    def point(p):
        for h in range(lines):
            q = p - 2 * h
            if 0 <= q < CHUNKS:
                @pl.when(on_line & (hop == h))
                def _(h=h, q=q):
                    if h > 0:
                        line_copy(q, 0).wait_recv()
                    pass_on(q)

    @pl.when(on_line & (hop == 0))
    def _():
        own = pltpu.make_async_copy(feat_ref, col_ref.at[slot], local_sem)
        own.start()
        own.wait()

    pivot = total[:FEAT]
    left = left_terms(pivot)
    right = right_terms(pivot)
    pleft_out[...] = left
    pright_out[...] = right
    point(0)
    point(1)
    eye = lax.broadcasted_iota(jnp.int32, (TILE, TILE), 1) == lax.broadcasted_iota(
        jnp.int32, (TILE, TILE), 0
    )
    table = jnp.exp(exponent(left, right)) + jnp.where(eye, total[FEAT : FEAT + 1], 0.0)
    inverse_out[...] = eliminate(table, lambda n: point(n + 2))
    for p in range(TILE // 8 + 2, CHUNKS + 2 * lines):
        point(p)
    for m in range(per_col):
        for q in range(CHUNKS):
            part = col_ref.at[m, pl.ds(q * rows_each, rows_each)]

            @pl.when(x != first_x + m)
            def _(m=m, q=q, part=part):
                pltpu.make_async_remote_copy(
                    src_ref=part, dst_ref=part, send_sem=side_send.at[0, q],
                    recv_sem=side_recv.at[m, q], device_id={"row": z * across + first_x + m},
                    device_id_type=MESH,
                ).wait_recv()
    for copy in nears + fars:
        copy.wait_send()
    for q in range(CHUNKS):
        @pl.when(up)
        def _(q=q):
            line_copy(q, 0).wait_send()

        @pl.when(down)
        def _(q=q):
            line_copy(q, 1).wait_send()

        @pl.when(on_line)
        def _(q=q):
            for d in range(1, across):
                side_copy(q, d).wait_send()


def panel_kernel(
    tiles, per_col, left_ref, noise_ref, here_ref, there_ref, pivot_ref, inverse_ref, pleft_ref,
    pright_ref, col_ref, out_panel, out_trailing, col_right, col_hi, col_lo,
):
    i = pl.program_id(0)
    lane = lax.broadcasted_iota(jnp.int32, (TILE, TILE), 1)
    sub = lax.broadcasted_iota(jnp.int32, (TILE, TILE), 0)
    width = tiles * TILE

    @pl.when(i == 0)
    def _():
        for m in range(per_col):
            cols = pl.ds(m * width, width)
            col_right[:, cols] = right_terms(col_ref[m])
            kern = jnp.exp(exponent(pleft_ref[...], col_right[:, cols]))
            panel = jnp.dot(
                inverse_ref[...], kern, precision=HIGHEST, preferred_element_type=jnp.float32
            )
            hi = panel.astype(jnp.bfloat16)
            col_hi[:, cols] = hi
            col_lo[:, cols] = (panel - hi.astype(jnp.float32)).astype(jnp.bfloat16)

    here = here_ref[pl.ds(pl.multiple_of(i * 8, 8), 1), :]
    pivot_tile = pivot_ref[0:1, :]
    left = left_ref[:, pl.ds(pl.multiple_of(i * TILE, TILE), TILE)]
    noise = jnp.where(lane == sub, noise_ref[pl.ds(i, 1), :], 0.0)
    kern = jnp.exp(exponent(left, pright_ref[...])) + jnp.where(here == pivot_tile, noise, 0.0)
    panel = lax.dot_general(
        kern, inverse_ref[...], CONTRACT_LAST, precision=HIGHEST, preferred_element_type=jnp.float32
    )
    panel = jnp.where(here >= pivot_tile, panel, 0.0)
    out_panel[...] = panel
    hi = panel.astype(jnp.bfloat16)
    lo = (panel - hi.astype(jnp.float32)).astype(jnp.bfloat16)
    row_terms = jnp.concatenate([hi, hi, lo], axis=1)
    for t in range(0, per_col * tiles, 2):
        cols = pl.ds(t * TILE, 2 * TILE)
        kern = jnp.exp(exponent(left, col_right[:, cols]))
        ch, cl = col_hi[:, cols], col_lo[:, cols]
        prod = jnp.dot(
            row_terms, jnp.concatenate([ch, cl, ch], axis=0), preferred_element_type=jnp.float32
        )
        value = kern - prod
        for u in range(2):
            there = there_ref[0:1, (t + u) * TILE : (t + u + 1) * TILE]
            live = (here >= there) & (there > pivot_tile)
            part = value[:, u * TILE : (u + 1) * TILE] + jnp.where(here == there, noise, 0.0)
            out_trailing[:, (t + u) * TILE : (t + u + 1) * TILE] = jnp.where(live, part, 0.0)


def shards(features, noise, tile_map, panel_tile):
    width = features.shape[0]
    tiles = width // TILE
    rows = lax.axis_size("row")
    cols = lax.axis_size("col")
    per_col = rows // cols
    across = 2 ** ((rows.bit_length() - 1) // 2)
    lines = rows // across
    slots = tile_map.shape[0]
    total = per_col * width
    hbm = pl.BlockSpec(memory_space=pltpu.HBM)
    vmem = pl.BlockSpec(memory_space=pltpu.VMEM)
    dma = pltpu.SemaphoreType.DMA
    f32, bf16, i32 = jnp.float32, jnp.bfloat16, jnp.int32
    shape = jax.ShapeDtypeStruct
    gathered = pl.pallas_call(
        functools.partial(gather_kernel, lines, across, cols, tiles),
        name="gather_and_factor",
        out_shape=(
            shape((DEPTH, width), bf16),
            shape((tiles, TILE), f32),
            shape((tiles * 8, TILE), i32),
            shape((8, total), i32),
            shape((8, TILE), i32),
            shape((TILE, TILE), f32),
            shape((DEPTH, TILE), bf16),
            shape((DEPTH, TILE), bf16),
            shape((per_col, FEAT, width), f32),
        ),
        in_specs=[hbm] * 4,
        out_specs=(vmem,) * 9,
        scratch_shapes=[
            pltpu.SMEM((slots,), i32),
            pltpu.SMEM((1,), i32),
            pltpu.VMEM((FEAT, width), f32),
            pltpu.VMEM((CAND, TILE), f32),
            pltpu.VMEM((CAND, TILE), f32),
            pltpu.VMEM((across - 1, CAND, TILE), f32),
            pltpu.VMEM((lines - 1, CAND, TILE), f32),
            dma((4,)),
            dma((across - 1,)),
            dma((across - 1,)),
            dma((lines - 1,)),
            dma((lines - 1,)),
            dma((2, CHUNKS)),
            dma((CHUNKS,)),
            dma((across - 1, CHUNKS)),
            dma((per_col, CHUNKS)),
            dma,
        ],
        compiler_params=pltpu.CompilerParams(
            collective_id=0, has_side_effects=True, vmem_limit_bytes=32 * 1024 * 1024
        ),
    )(tile_map, panel_tile, features.T, noise.reshape(tiles, TILE))
    return pl.pallas_call(
        functools.partial(panel_kernel, tiles, per_col),
        name="panel_and_trailing",
        grid=(tiles,),
        out_shape=(shape((width, TILE), f32), shape((width, total), f32)),
        in_specs=[vmem] * 9,
        out_specs=(
            pl.BlockSpec((TILE, TILE), lambda i: (i, 0)),
            pl.BlockSpec((TILE, total), lambda i: (i, 0)),
        ),
        scratch_shapes=[
            pltpu.VMEM((DEPTH, total), bf16),
            pltpu.VMEM((TILE, total), bf16),
            pltpu.VMEM((TILE, total), bf16),
        ],
        compiler_params=pltpu.CompilerParams(vmem_limit_bytes=48 * 1024 * 1024),
    )(*gathered)


def solution(mesh):
    in_specs = (P("row", None), P("row"), P(), P())
    out_specs = (P("row", None), P("row", "col"))
    return jax.shard_map(shards, mesh=mesh, in_specs=in_specs, out_specs=out_specs, check_vma=False)
```

profile of v0, /device:TPU:4, one launch (start us, length us, event | category | flops | bytes accessed | tf_op | source)
XLA Modules:
  0.0 40.9 jit_solution(5256615875687620446)
XLA Ops:
  1.3 0.0 copy-start
  1.3 0.9 %copy-done = f32[768,64]{0,1:T(8,128)S(1)} copy-done((f32[768,64]{0,1:T(8,128)S(1)}, f32[768,64]{0,1:T(8,128)}, u32[]{:S(2)}) %copy-start) | copy-done | bytes 196632
  2.2 0.0 copy-start.1
  2.2 0.7 %copy-done.1 = f32[768]{0:T(1024)S(1)} copy-done((f32[768]{0:T(1024)S(1)}, f32[768]{0:T(1024)}, u32[]{:S(2)}) %copy-start.1) | copy-done | bytes 3096
  2.9 0.0 copy-start.2
  2.9 0.7 %copy-done.2 = s32[48]{0:T(128)S(1)} copy-done((s32[48]{0:T(128)S(1)}, s32[48]{0:T(128)}, u32[]{:S(2)}) %copy-start.2) | copy-done | bytes 216
  3.5 29.0 %gather_and_factor.1 = (bf16[400,768]{1,0:T(8,128)(2,1)S(1)}, f32[6,128]{1,0:T(8,128)S(1)}, s32[48,128]{1,0:T(8,128)S(1)}, s32[8,1536]{1,0:T(8,128)S(1)}, s32[8,...) custom-call(s32[48]{0:T(128)S(1)} %copy-done.2, ...), custom_call_target="tpu_custom_call" | custom-call | tf_op jit(solution)/shard_map/gather_and_factor/pallas_call | solution.py:340
  32.5 8.3 %panel_and_trailing.1 = (f32[768,128]{1,0:T(8,128)}, f32[768,1536]{1,0:T(8,128)}) custom-call(bf16[400,768]{1,0:T(8,128)(2,1)S(1)} %get-tuple-element.11.left_ref, f32[6,128]{1,0:T(8,128)S(1)} %get-tuple-element.12.noise_ref, s32[48,128]{1,0:T(8,128)S(1)} %get-tuple-element.13.here_ref, s32[8,1536]{1,0:T(8,128)S(1)} %get-tuple-element.14.there_ref, ...), custom_call_target="tpu_custom_call" | custom-call | tf_op jit(solution)/shard_map/panel_and_trailing/pallas_call | solution.py:379
Async XLA Ops:
  1.3 0.9 %copy-start = (f32[768,64]{0,1:T(8,128)S(1)}, f32[768,64]{0,1:T(8,128)}, u32[]{:S(2)}) copy-start(f32[768,64]{0,1:T(8,128)} %param.4) | copy-start | bytes 589828
  2.2 0.7 %copy-start.1 = (f32[768]{0:T(1024)S(1)}, f32[768]{0:T(1024)}, u32[]{:S(2)}) copy-start(f32[768]{0:T(1024)} %param.5) | copy-start | bytes 9220
  2.9 0.7 %copy-start.2 = (s32[48]{0:T(128)S(1)}, s32[48]{0:T(128)}, u32[]{:S(2)}) copy-start(s32[48]{0:T(128)} %map_hbm.1) | copy-start | bytes 580
where the time goes:
time: 41.1 us; the launch traced here: 40.9 us
  Pallas kernels  37.3 us (91%)
  local copies, waits for them, and re-layouts  2.26 us (5%)
  between operations  1.3 us (3%)
    pallas_call x1, Pallas kernels, shards(): pl.pallas_call(functools.partial(gather_kernel, lines, across, cols, tile...  29 us
    pallas_call x1, Pallas kernels, shards(): pl.pallas_call(functools.partial(panel_kernel, tiles, per_col), name='pan...  8.31 us
    unnamed x6, local copies, waits for them, and re-layouts  2.26 us

commit v1 on v0

--- a/solution.py
+++ b/solution.py
@@ -52,38 +52,63 @@
 
 
 def eliminate(table, between=None):
-    lane = lax.broadcasted_iota(jnp.int32, (1, TILE), 1)
-    sub = lax.broadcasted_iota(jnp.int32, (8, 1), 0)
+    lane = lax.broadcasted_iota(jnp.int32, (8, TILE), 1)
+    sub = lax.broadcasted_iota(jnp.int32, (8, TILE), 0)
     block_lane = lax.broadcasted_iota(jnp.int32, (BLOCK, TILE), 1)
     block_sub = lax.broadcasted_iota(jnp.int32, (BLOCK, TILE), 0)
+    full = (8, TILE)
     done = []
     below = table
     for k in range(TILE // BLOCK):
         groups = [below[g * 8 : g * 8 + 8] for g in range(BLOCK // 8)]
         pieces = []
-        for j in range(BLOCK):
-            at = k * BLOCK + j
-            g, o = j // 8, j % 8
-            row = groups[g][o : o + 1]
-            pivot = row[:, at : at + 1]
-            unit = jnp.where(lane == at, 1.0, row)
-            pieces.append(unit / jnp.sqrt(pivot))
-            scaled = unit / pivot
-            for h in range(g, BLOCK // 8):
-                col = groups[h][:, at : at + 1]
-                if h == g:
-                    col = jnp.where(sub > o, col, 0.0)
-                    keep = (lane != at) | (sub <= o)
-                else:
-                    keep = lane != at
-                groups[h] = jnp.where(keep, groups[h], 0.0) - col * scaled
-            if between is not None and j % 8 == 7:
+        for g in range(BLOCK // 8):
+            at = k * BLOCK + g * 8
+            own = (lane >= at) & (lane < at + 8)
+            here = groups[g]
+            wide = [jnp.broadcast_to(here[:, at + j : at + j + 1], full) for j in range(8)]
+            entry = {
+                (i, j): jnp.broadcast_to(wide[j][i : i + 1], full)
+                for i in range(8) for j in range(i + 1)
+            }
+            row = [
+                jnp.where(
+                    own, jnp.where(lane == at + i, 1.0, 0.0), jnp.broadcast_to(here[i : i + 1], full)
+                )
+                for i in range(8)
+            ]
+            later = range(g + 1, BLOCK // 8)
+            cols = {
+                h: [jnp.broadcast_to(groups[h][:, at + j : at + j + 1], full) for j in range(8)]
+                for h in later
+            }
+            piece = jnp.zeros(full, jnp.float32)
+            rest = {h: jnp.where(own, 0.0, groups[h]) for h in later}
+            for j in range(8):
+                pivot = entry[j, j]
+                inv = 1.0 / pivot
+                factor = [entry[i, j] * inv for i in range(j + 1, 8)]
+                for i in range(j + 1, 8):
+                    for l in range(j + 1, i + 1):
+                        entry[i, l] = entry[i, l] - factor[i - j - 1] * entry[l, j]
+                scaled = row[j] * inv
+                for i in range(j + 1, 8):
+                    row[i] = row[i] - entry[i, j] * scaled
+                piece = jnp.where(sub == j, row[j] / jnp.sqrt(pivot), piece)
+                for h in later:
+                    for l in range(j + 1, 8):
+                        cols[h][l] = cols[h][l] - cols[h][j] * factor[l - j - 1]
+                    rest[h] = rest[h] - cols[h][j] * scaled
+            for h in later:
+                groups[h] = rest[h]
+            pieces.append(piece)
+            if between is not None:
                 between(at // 8)
         block = jnp.concatenate(pieces, axis=0)
         lower = block_lane <= block_sub + k * BLOCK
         done.append(jnp.where(lower, block, 0.0))
         if (k + 1) * BLOCK < TILE:
-            own = (lane >= k * BLOCK) & (lane < (k + 1) * BLOCK)
+            own = (lane[:1] >= k * BLOCK) & (lane[:1] < (k + 1) * BLOCK)
             right = jnp.where(lower | (block_lane >= (k + 1) * BLOCK), block, 0.0)
             update = lax.dot_general(
                 block, right, CONTRACT_FIRST, precision=HIGHEST, preferred_element_type=jnp.float32
@@ -96,9 +121,9 @@
 
 
 def gather_kernel(
-    lines, across, cols, tiles, map_hbm, panel_hbm, feat_hbm, noise_hbm,
+    lines, across, cols, tiles, map_hbm, panel_ref, feat_hbm, noise_hbm,
     left_out, noise_out, here_out, there_out, pivot_out, inverse_out, pleft_out, pright_out, col_ref,
-    map_ref, panel_ref, feat_ref, own_ref, sum_ref, near_ref, far_ref,
+    map_ref, feat_ref, own_ref, sum_ref, near_ref, far_ref,
     in_sem, near_send, near_recv, far_send, far_recv, line_send, line_recv, side_send, side_recv, local_sem,
 ):
     r = lax.axis_index("row")
@@ -110,7 +135,7 @@
     loads = [
         pltpu.make_async_copy(src, dst, in_sem.at[n])
         for n, (src, dst) in enumerate(
-            [(map_hbm, map_ref), (panel_hbm, panel_ref), (feat_hbm, feat_ref), (noise_hbm, noise_out)]
+            [(map_hbm, map_ref), (feat_hbm, feat_ref), (noise_hbm, noise_out)]
         )
     ]
     for load in loads:
@@ -152,7 +177,7 @@
     for copy in nears:
         copy.start()
     for s in range(tiles):
-        left_out[:, s * TILE : (s + 1) * TILE] = left_terms(feat_ref[:, s * TILE : (s + 1) * TILE])
+        left_out[s * TILE : (s + 1) * TILE] = left_terms(feat_ref[:, s * TILE : (s + 1) * TILE]).T
         here_out[s * 8 : s * 8 + 8] = jnp.full((8, TILE), map_ref[r * tiles + s], jnp.int32)
     for t in range(per_col * tiles):
         there_out[:, t * TILE : (t + 1) * TILE] = jnp.full(
@@ -167,11 +192,6 @@
     sum_ref[...] = total
     for copy in fars:
         copy.start()
-    for copy in fars:
-        copy.wait_recv()
-    for d in range(1, lines):
-        total += far_ref[d - 1]
-
     first = c * per_col
     source_z = first // across
     first_x = lax.rem(first, across)
@@ -230,13 +250,17 @@
         own.start()
         own.wait()
 
+    point(0)
+    point(1)
+    for copy in fars:
+        copy.wait_recv()
+    for d in range(1, lines):
+        total += far_ref[d - 1]
     pivot = total[:FEAT]
     left = left_terms(pivot)
     right = right_terms(pivot)
     pleft_out[...] = left
     pright_out[...] = right
-    point(0)
-    point(1)
     eye = lax.broadcasted_iota(jnp.int32, (TILE, TILE), 1) == lax.broadcasted_iota(
         jnp.int32, (TILE, TILE), 0
     )
@@ -273,53 +297,57 @@
 
 
 def panel_kernel(
-    tiles, per_col, left_ref, noise_ref, here_ref, there_ref, pivot_ref, inverse_ref, pleft_ref,
-    pright_ref, col_ref, out_panel, out_trailing, col_right, col_hi, col_lo,
+    tiles, left_ref, noise_ref, here_ref, there_ref, pivot_ref, inverse_ref, pleft_ref,
+    pright_ref, col_ref, out_panel, out_trailing, row_terms,
 ):
-    i = pl.program_id(0)
     lane = lax.broadcasted_iota(jnp.int32, (TILE, TILE), 1)
     sub = lax.broadcasted_iota(jnp.int32, (TILE, TILE), 0)
-    width = tiles * TILE
-
-    @pl.when(i == 0)
+    pivot_tile = pivot_ref[0:1, :]
+    inverse = inverse_ref[...]
+
+    def tile_of(i):
+        here = here_ref[i * 8 : i * 8 + 1, :]
+        return here, jnp.where(lane == sub, noise_ref[i : i + 1, :], 0.0)
+
+    @pl.when(pl.program_id(0) == 0)
     def _():
-        for m in range(per_col):
-            cols = pl.ds(m * width, width)
-            col_right[:, cols] = right_terms(col_ref[m])
-            kern = jnp.exp(exponent(pleft_ref[...], col_right[:, cols]))
-            panel = jnp.dot(
-                inverse_ref[...], kern, precision=HIGHEST, preferred_element_type=jnp.float32
-            )
-            hi = panel.astype(jnp.bfloat16)
-            col_hi[:, cols] = hi
-            col_lo[:, cols] = (panel - hi.astype(jnp.float32)).astype(jnp.bfloat16)
-
-    here = here_ref[pl.ds(pl.multiple_of(i * 8, 8), 1), :]
-    pivot_tile = pivot_ref[0:1, :]
-    left = left_ref[:, pl.ds(pl.multiple_of(i * TILE, TILE), TILE)]
-    noise = jnp.where(lane == sub, noise_ref[pl.ds(i, 1), :], 0.0)
-    kern = jnp.exp(exponent(left, pright_ref[...])) + jnp.where(here == pivot_tile, noise, 0.0)
-    panel = lax.dot_general(
-        kern, inverse_ref[...], CONTRACT_LAST, precision=HIGHEST, preferred_element_type=jnp.float32
-    )
-    panel = jnp.where(here >= pivot_tile, panel, 0.0)
-    out_panel[...] = panel
+        kern = jnp.exp(jnp.dot(left_ref[...], pright_ref[...], preferred_element_type=jnp.float32))
+        parts = []
+        for i in range(tiles):
+            here, noise = tile_of(i)
+            part = kern[i * TILE : (i + 1) * TILE]
+            parts.append(part + jnp.where(here == pivot_tile, noise, 0.0))
+        panel = lax.dot_general(
+            jnp.concatenate(parts, axis=0), inverse, CONTRACT_LAST,
+            precision=HIGHEST, preferred_element_type=jnp.float32,
+        )
+        for i in range(tiles):
+            rows = slice(i * TILE, (i + 1) * TILE)
+            part = jnp.where(tile_of(i)[0] >= pivot_tile, panel[rows], 0.0)
+            out_panel[rows] = part
+            hi = part.astype(jnp.bfloat16)
+            row_terms[rows, :TILE] = hi
+            row_terms[rows, TILE : 2 * TILE] = hi
+            row_terms[rows, 2 * TILE :] = (part - hi.astype(jnp.float32)).astype(jnp.bfloat16)
+
+    right = right_terms(col_ref[0])
+    kern = jnp.exp(exponent(pleft_ref[...], right))
+    panel = jnp.dot(inverse, kern, precision=HIGHEST, preferred_element_type=jnp.float32)
     hi = panel.astype(jnp.bfloat16)
     lo = (panel - hi.astype(jnp.float32)).astype(jnp.bfloat16)
-    row_terms = jnp.concatenate([hi, hi, lo], axis=1)
-    for t in range(0, per_col * tiles, 2):
-        cols = pl.ds(t * TILE, 2 * TILE)
-        kern = jnp.exp(exponent(left, col_right[:, cols]))
-        ch, cl = col_hi[:, cols], col_lo[:, cols]
-        prod = jnp.dot(
-            row_terms, jnp.concatenate([ch, cl, ch], axis=0), preferred_element_type=jnp.float32
-        )
-        value = kern - prod
+    col_terms = jnp.concatenate([hi, lo, hi], axis=0)
+    value = jnp.exp(jnp.dot(left_ref[...], right, preferred_element_type=jnp.float32)) - jnp.dot(
+        row_terms[...], col_terms, preferred_element_type=jnp.float32
+    )
+    for i in range(tiles):
+        here, noise = tile_of(i)
+        rows = slice(i * TILE, (i + 1) * TILE)
         for u in range(2):
-            there = there_ref[0:1, (t + u) * TILE : (t + u + 1) * TILE]
+            cols = slice(u * TILE, (u + 1) * TILE)
+            there = there_ref[0:1, cols]
             live = (here >= there) & (there > pivot_tile)
-            part = value[:, u * TILE : (u + 1) * TILE] + jnp.where(here == there, noise, 0.0)
-            out_trailing[:, (t + u) * TILE : (t + u + 1) * TILE] = jnp.where(live, part, 0.0)
+            part = value[rows, cols] + jnp.where(here == there, noise, 0.0)
+            out_trailing[rows, cols] = jnp.where(live, part, 0.0)
 
 
 def shards(features, noise, tile_map, panel_tile):
@@ -332,6 +360,7 @@
     lines = rows // across
     slots = tile_map.shape[0]
     total = per_col * width
+    smem = pl.BlockSpec(memory_space=pltpu.SMEM)
     hbm = pl.BlockSpec(memory_space=pltpu.HBM)
     vmem = pl.BlockSpec(memory_space=pltpu.VMEM)
     dma = pltpu.SemaphoreType.DMA
@@ -341,7 +370,7 @@
         functools.partial(gather_kernel, lines, across, cols, tiles),
         name="gather_and_factor",
         out_shape=(
-            shape((DEPTH, width), bf16),
+            shape((width, DEPTH), bf16),
             shape((tiles, TILE), f32),
             shape((tiles * 8, TILE), i32),
             shape((8, total), i32),
@@ -351,17 +380,16 @@
             shape((DEPTH, TILE), bf16),
             shape((per_col, FEAT, width), f32),
         ),
-        in_specs=[hbm] * 4,
+        in_specs=[hbm, smem, hbm, hbm],
         out_specs=(vmem,) * 9,
         scratch_shapes=[
             pltpu.SMEM((slots,), i32),
-            pltpu.SMEM((1,), i32),
             pltpu.VMEM((FEAT, width), f32),
             pltpu.VMEM((CAND, TILE), f32),
             pltpu.VMEM((CAND, TILE), f32),
             pltpu.VMEM((across - 1, CAND, TILE), f32),
             pltpu.VMEM((lines - 1, CAND, TILE), f32),
-            dma((4,)),
+            dma((3,)),
             dma((across - 1,)),
             dma((across - 1,)),
             dma((lines - 1,)),
@@ -375,22 +403,28 @@
         compiler_params=pltpu.CompilerParams(
             collective_id=0, has_side_effects=True, vmem_limit_bytes=32 * 1024 * 1024
         ),
-    )(tile_map, panel_tile, features.T, noise.reshape(tiles, TILE))
+    )(
+        pltpu.with_memory_space_constraint(tile_map, pltpu.HBM),
+        panel_tile,
+        pltpu.with_memory_space_constraint(features.T, pltpu.HBM),
+        pltpu.with_memory_space_constraint(noise.reshape(tiles, TILE), pltpu.HBM),
+    )
+    step = 2 * TILE
+    each = width // step
     return pl.pallas_call(
-        functools.partial(panel_kernel, tiles, per_col),
+        functools.partial(panel_kernel, tiles),
         name="panel_and_trailing",
-        grid=(tiles,),
+        grid=(per_col * each,),
         out_shape=(shape((width, TILE), f32), shape((width, total), f32)),
-        in_specs=[vmem] * 9,
+        in_specs=[vmem] * 3
+        + [pl.BlockSpec((8, step), lambda i: (0, i))]
+        + [vmem] * 4
+        + [pl.BlockSpec((1, FEAT, step), lambda i: (i // each, 0, i % each))],
         out_specs=(
-            pl.BlockSpec((TILE, TILE), lambda i: (i, 0)),
-            pl.BlockSpec((TILE, total), lambda i: (i, 0)),
+            pl.BlockSpec((width, TILE), lambda i: (0, 0)),
+            pl.BlockSpec((width, step), lambda i: (0, i)),
         ),
-        scratch_shapes=[
-            pltpu.VMEM((DEPTH, total), bf16),
-            pltpu.VMEM((TILE, total), bf16),
-            pltpu.VMEM((TILE, total), bf16),
-        ],
+        scratch_shapes=[pltpu.VMEM((width, 3 * TILE), bf16)],
         compiler_params=pltpu.CompilerParams(vmem_limit_bytes=48 * 1024 * 1024),
     )(*gathered)
 

time: 41.1 us -> 33.6 us (0.82)
  Pallas kernels: 37.3 us -> 32 us
  local copies, waits for them, and re-layouts: 2.26 us -> 0 us
    pallas_call x1, Pallas kernels: 29 us -> 23.4 us  [shards(): pl.pallas_call(functools.partial(gather_kernel, lines, across, cols, tile...]
    unnamed x6 -> x0, local copies, waits for them, and re-layouts: 2.26 us -> none
where the time goes in v1:
time: 33.6 us; the launch traced here: 33.3 us
  Pallas kernels  32 us (95%)
  between operations  1.28 us (4%)
    pallas_call x1, Pallas kernels, shards(): pl.pallas_call(functools.partial(gather_kernel, lines, across, cols, tile...  23.4 us
    pallas_call x1, Pallas kernels, shards(): pl.pallas_call(functools.partial(panel_kernel, tiles), name='panel_and_tr...  8.61 us

profile of v1, /device:TPU:4, one launch (start us, length us, event | category | flops | bytes accessed | tf_op | source)
XLA Modules:
  0.0 33.3 jit_solution(14523489887852829715)
XLA Ops:
  1.3 23.4 %gather_and_factor.1 = (bf16[768,400]{1,0:T(8,128)(2,1)S(1)}, f32[6,128]{1,0:T(8,128)S(1)}, s32[48,128]{1,0:T(8,128)S(1)}, s32[8,1536]{1,0:T(8,128)S(1)}, s32[8,...) custom-call(s32[48]{0:T(128)} %map_hbm.1, ...), custom_call_target="tpu_custom_call" | custom-call | tf_op jit(solution)/shard_map/gather_and_factor/pallas_call | solution.py:369
  24.7 8.6 %panel_and_trailing.1 = (f32[768,128]{1,0:T(8,128)}, f32[768,1536]{1,0:T(8,128)}) custom-call(bf16[768,400]{1,0:T(8,128)(2,1)S(1)} %get-tuple-element.11.left_ref, f32[6,128]{1,0:T(8,128)S(1)} %get-tuple-element.12.noise_ref, s32[48,128]{1,0:T(8,128)S(1)} %get-tuple-element.13.here_ref, s32[8,1536]{1,0:T(8,128)S(1)} %get-tuple-element.14.there_ref, ...), custom_call_target="tpu_custom_call" | custom-call | tf_op jit(solution)/shard_map/panel_and_trailing/pallas_call | solution.py:414

commit v2 on v1

--- a/solution.py
+++ b/solution.py
@@ -122,7 +122,7 @@
 
 def gather_kernel(
     lines, across, cols, tiles, map_hbm, panel_ref, feat_hbm, noise_hbm,
-    left_out, noise_out, here_out, there_out, pivot_out, inverse_out, pleft_out, pright_out, col_ref,
+    left_out, noise_out, here_out, there_out, pivot_out, inverse_out, pleft_out, kern_out, col_ref,
     map_ref, feat_ref, own_ref, sum_ref, near_ref, far_ref,
     in_sem, near_send, near_recv, far_send, far_recv, line_send, line_recv, side_send, side_recv, local_sem,
 ):
@@ -176,14 +176,6 @@
     fars = [far(d) for d in range(1, lines)]
     for copy in nears:
         copy.start()
-    for s in range(tiles):
-        left_out[s * TILE : (s + 1) * TILE] = left_terms(feat_ref[:, s * TILE : (s + 1) * TILE]).T
-        here_out[s * 8 : s * 8 + 8] = jnp.full((8, TILE), map_ref[r * tiles + s], jnp.int32)
-    for t in range(per_col * tiles):
-        there_out[:, t * TILE : (t + 1) * TILE] = jnp.full(
-            (8, TILE), map_ref[c * per_col * tiles + t], jnp.int32
-        )
-    pivot_out[...] = jnp.full((8, TILE), pivot_tile, jnp.int32)
     for copy in nears:
         copy.wait_recv()
     total = own_ref[...]
@@ -260,12 +252,31 @@
     left = left_terms(pivot)
     right = right_terms(pivot)
     pleft_out[...] = left
-    pright_out[...] = right
     eye = lax.broadcasted_iota(jnp.int32, (TILE, TILE), 1) == lax.broadcasted_iota(
         jnp.int32, (TILE, TILE), 0
     )
     table = jnp.exp(exponent(left, right)) + jnp.where(eye, total[FEAT : FEAT + 1], 0.0)
-    inverse_out[...] = eliminate(table, lambda n: point(n + 2))
+
+    def beside(n):
+        if n < tiles:
+            rows = slice(n * TILE, (n + 1) * TILE)
+            left_out[rows] = left_terms(feat_ref[:, rows]).T
+            here_out[n * 8 : n * 8 + 8] = jnp.full((8, TILE), map_ref[r * tiles + n], jnp.int32)
+        elif n < 2 * tiles:
+            s = n - tiles
+            rows = slice(s * TILE, (s + 1) * TILE)
+            kern = jnp.exp(jnp.dot(left_out[rows], right, preferred_element_type=jnp.float32))
+            held = map_ref[r * tiles + s] == pivot_tile
+            kern_out[rows] = kern + jnp.where(eye & held, noise_out[s : s + 1], 0.0)
+        elif n == 2 * tiles:
+            for t in range(per_col * tiles):
+                there_out[:, t * TILE : (t + 1) * TILE] = jnp.full(
+                    (8, TILE), map_ref[c * per_col * tiles + t], jnp.int32
+                )
+            pivot_out[...] = jnp.full((8, TILE), pivot_tile, jnp.int32)
+        point(n + 2)
+
+    inverse_out[...] = eliminate(table, beside)
     for p in range(TILE // 8 + 2, CHUNKS + 2 * lines):
         point(p)
     for m in range(per_col):
@@ -298,7 +309,7 @@
 
 def panel_kernel(
     tiles, left_ref, noise_ref, here_ref, there_ref, pivot_ref, inverse_ref, pleft_ref,
-    pright_ref, col_ref, out_panel, out_trailing, row_terms,
+    kern_ref, col_ref, out_panel, out_trailing, row_terms, right_ref, col_terms,
 ):
     lane = lax.broadcasted_iota(jnp.int32, (TILE, TILE), 1)
     sub = lax.broadcasted_iota(jnp.int32, (TILE, TILE), 0)
@@ -311,14 +322,8 @@
 
     @pl.when(pl.program_id(0) == 0)
     def _():
-        kern = jnp.exp(jnp.dot(left_ref[...], pright_ref[...], preferred_element_type=jnp.float32))
-        parts = []
-        for i in range(tiles):
-            here, noise = tile_of(i)
-            part = kern[i * TILE : (i + 1) * TILE]
-            parts.append(part + jnp.where(here == pivot_tile, noise, 0.0))
         panel = lax.dot_general(
-            jnp.concatenate(parts, axis=0), inverse, CONTRACT_LAST,
+            kern_ref[...], inverse, CONTRACT_LAST,
             precision=HIGHEST, preferred_element_type=jnp.float32,
         )
         for i in range(tiles):
@@ -330,15 +335,22 @@
             row_terms[rows, TILE : 2 * TILE] = hi
             row_terms[rows, 2 * TILE :] = (part - hi.astype(jnp.float32)).astype(jnp.bfloat16)
 
-    right = right_terms(col_ref[0])
-    kern = jnp.exp(exponent(pleft_ref[...], right))
-    panel = jnp.dot(inverse, kern, precision=HIGHEST, preferred_element_type=jnp.float32)
-    hi = panel.astype(jnp.bfloat16)
-    lo = (panel - hi.astype(jnp.float32)).astype(jnp.bfloat16)
-    col_terms = jnp.concatenate([hi, lo, hi], axis=0)
-    value = jnp.exp(jnp.dot(left_ref[...], right, preferred_element_type=jnp.float32)) - jnp.dot(
-        row_terms[...], col_terms, preferred_element_type=jnp.float32
-    )
+        for m in range(col_ref.shape[0]):
+            right = right_terms(col_ref[m])
+            cols = slice(m * tiles * TILE, (m + 1) * tiles * TILE)
+            right_ref[:, cols] = right
+            kern = jnp.exp(exponent(pleft_ref[...], right))
+            part = jnp.dot(inverse, kern, precision=HIGHEST, preferred_element_type=jnp.float32)
+            hi = part.astype(jnp.bfloat16)
+            col_terms[:TILE, cols] = hi
+            col_terms[TILE : 2 * TILE, cols] = (part - hi.astype(jnp.float32)).astype(jnp.bfloat16)
+            col_terms[2 * TILE :, cols] = hi
+
+    step = out_trailing.shape[1]
+    now = pl.ds(pl.multiple_of(pl.program_id(0) * step, step), step)
+    value = jnp.exp(
+        jnp.dot(left_ref[...], right_ref[:, now], preferred_element_type=jnp.float32)
+    ) - jnp.dot(row_terms[...], col_terms[:, now], preferred_element_type=jnp.float32)
     for i in range(tiles):
         here, noise = tile_of(i)
         rows = slice(i * TILE, (i + 1) * TILE)
@@ -377,7 +389,7 @@
             shape((8, TILE), i32),
             shape((TILE, TILE), f32),
             shape((DEPTH, TILE), bf16),
-            shape((DEPTH, TILE), bf16),
+            shape((width, TILE), f32),
             shape((per_col, FEAT, width), f32),
         ),
         in_specs=[hbm, smem, hbm, hbm],
@@ -410,21 +422,23 @@
         pltpu.with_memory_space_constraint(noise.reshape(tiles, TILE), pltpu.HBM),
     )
     step = 2 * TILE
-    each = width // step
     return pl.pallas_call(
         functools.partial(panel_kernel, tiles),
         name="panel_and_trailing",
-        grid=(per_col * each,),
+        grid=(total // step,),
         out_shape=(shape((width, TILE), f32), shape((width, total), f32)),
         in_specs=[vmem] * 3
         + [pl.BlockSpec((8, step), lambda i: (0, i))]
-        + [vmem] * 4
-        + [pl.BlockSpec((1, FEAT, step), lambda i: (i // each, 0, i % each))],
+        + [vmem] * 5,
         out_specs=(
             pl.BlockSpec((width, TILE), lambda i: (0, 0)),
             pl.BlockSpec((width, step), lambda i: (0, i)),
         ),
-        scratch_shapes=[pltpu.VMEM((width, 3 * TILE), bf16)],
+        scratch_shapes=[
+            pltpu.VMEM((width, 3 * TILE), bf16),
+            pltpu.VMEM((DEPTH, total), bf16),
+            pltpu.VMEM((3 * TILE, total), bf16),
+        ],
         compiler_params=pltpu.CompilerParams(vmem_limit_bytes=48 * 1024 * 1024),
     )(*gathered)
 

time: 33.6 us -> 31.7 us (0.943)
  Pallas kernels: 32 us -> 30.1 us
    pallas_call x1, Pallas kernels: 8.61 us -> 6.57 us  [shards(): pl.pallas_call(functools.partial(panel_kernel, tiles), name='panel_and_tr...]
where the time goes in v2:
time: 31.7 us; the launch traced here: 31.4 us
  Pallas kernels  30.1 us (95%)
  between operations  1.28 us (4%)
    pallas_call x1, Pallas kernels, shards(): pl.pallas_call(functools.partial(gather_kernel, lines, across, cols, tile...  23.5 us
    pallas_call x1, Pallas kernels, shards(): pl.pallas_call(functools.partial(panel_kernel, tiles), name='panel_and_tr...  6.57 us

profile of v2, /device:TPU:4, one launch (start us, length us, event | category | flops | bytes accessed | tf_op | source)
XLA Modules:
  0.0 31.4 jit_solution(14349533677553729261)
XLA Ops:
  1.3 23.5 %gather_and_factor.1 = (bf16[768,400]{1,0:T(8,128)(2,1)S(1)}, f32[6,128]{1,0:T(8,128)S(1)}, s32[48,128]{1,0:T(8,128)S(1)}, s32[8,1536]{1,0:T(8,128)S(1)}, s32[8,...) custom-call(s32[48]{0:T(128)} %map_hbm.1, ...), custom_call_target="tpu_custom_call" | custom-call | tf_op jit(solution)/shard_map/gather_and_factor/pallas_call | solution.py:381
  24.8 6.6 %panel_and_trailing.1 = (f32[768,128]{1,0:T(8,128)}, f32[768,1536]{1,0:T(8,128)}) custom-call(bf16[768,400]{1,0:T(8,128)(2,1)S(1)} %get-tuple-element.11.left_ref, f32[6,128]{1,0:T(8,128)S(1)} %get-tuple-element.12.noise_ref, s32[48,128]{1,0:T(8,128)S(1)} %get-tuple-element.13.here_ref, s32[8,1536]{1,0:T(8,128)S(1)} %get-tuple-element.14.there_ref, ...), custom_call_target="tpu_custom_call" | custom-call | tf_op jit(solution)/shard_map/panel_and_trailing/pallas_call | solution.py:425

commit v3 on v2

--- a/solution.py
+++ b/solution.py
@@ -118,6 +118,7 @@
 
 
 CHUNKS = 4
+LAG = 4
 
 
 def gather_kernel(
@@ -228,7 +229,7 @@
 
     def point(p):
         for h in range(lines):
-            q = p - 2 * h
+            q = p - LAG * h
             if 0 <= q < CHUNKS:
                 @pl.when(on_line & (hop == h))
                 def _(h=h, q=q):
@@ -242,8 +243,8 @@
         own.start()
         own.wait()
 
-    point(0)
-    point(1)
+    for p in range(LAG):
+        point(p)
     for copy in fars:
         copy.wait_recv()
     for d in range(1, lines):
@@ -274,10 +275,10 @@
                     (8, TILE), map_ref[c * per_col * tiles + t], jnp.int32
                 )
             pivot_out[...] = jnp.full((8, TILE), pivot_tile, jnp.int32)
-        point(n + 2)
+        point(n + LAG)
 
     inverse_out[...] = eliminate(table, beside)
-    for p in range(TILE // 8 + 2, CHUNKS + 2 * lines):
+    for p in range(TILE // 8 + LAG, CHUNKS + LAG * lines):
         point(p)
     for m in range(per_col):
         for q in range(CHUNKS):

time: 31.7 us -> 30 us (0.946)
  Pallas kernels: 30.1 us -> 28.2 us
    pallas_call x1, Pallas kernels: 23.5 us -> 21.7 us  [shards(): pl.pallas_call(functools.partial(gather_kernel, lines, across, cols, tile...]
where the time goes in v3:
time: 30 us; the launch traced here: 29.5 us
  Pallas kernels  28.2 us (94%)
  between operations  1.28 us (4%)
    pallas_call x1, Pallas kernels, shards(): pl.pallas_call(functools.partial(gather_kernel, lines, across, cols, tile...  21.7 us
    pallas_call x1, Pallas kernels, shards(): pl.pallas_call(functools.partial(panel_kernel, tiles), name='panel_and_tr...  6.57 us

profile of v3, /device:TPU:4, one launch (start us, length us, event | category | flops | bytes accessed | tf_op | source)
XLA Modules:
  0.0 29.5 jit_solution(4616629985330626180)
XLA Ops:
  1.3 21.7 %gather_and_factor.1 = (bf16[768,400]{1,0:T(8,128)(2,1)S(1)}, f32[6,128]{1,0:T(8,128)S(1)}, s32[48,128]{1,0:T(8,128)S(1)}, s32[8,1536]{1,0:T(8,128)S(1)}, s32[8,...) custom-call(s32[48]{0:T(128)} %map_hbm.1, ...), custom_call_target="tpu_custom_call" | custom-call | tf_op jit(solution)/shard_map/gather_and_factor/pallas_call | solution.py:382
  23.0 6.6 %panel_and_trailing.1 = (f32[768,128]{1,0:T(8,128)}, f32[768,1536]{1,0:T(8,128)}) custom-call(bf16[768,400]{1,0:T(8,128)(2,1)S(1)} %get-tuple-element.11.left_ref, f32[6,128]{1,0:T(8,128)S(1)} %get-tuple-element.12.noise_ref, s32[48,128]{1,0:T(8,128)S(1)} %get-tuple-element.13.here_ref, s32[8,1536]{1,0:T(8,128)S(1)} %get-tuple-element.14.there_ref, ...), custom_call_target="tpu_custom_call" | custom-call | tf_op jit(solution)/shard_map/panel_and_trailing/pallas_call | solution.py:426
